TPU v7x, 512 devices: a whole 4x4x16 slice. The times are simulated.
512 devices in a mesh: row: 16 (over y, z_hi), col: 32 (over z_lo, x, core).
Axes of the slice: x: 4, y: 4, z: 16 (z_hi: 4, z_lo: 4; z = z_hi * 4 + z_lo), core: 2. Of those that a mesh axis runs over, the one named last changes fastest.
Arguments:
- vectors: bfloat16 [49152, 128], P('row'), may hold values from -6 to 6
- tiles: bfloat16 [4096, 256, 256], P(('row', 'col')), may hold values from -0.0546875 to 0.0546875
- tile_rows: int32 [4096], P(('row', 'col')), may hold values from 0 to 191, as said below
- tile_cols: int32 [4096], P(('row', 'col')), may hold values from 0 to 191, as said below
Outputs:
- applied: bfloat16 [49152, 128], P(('row', 'col'))
- applied_twice: bfloat16 [49152, 128], P(('row', 'col'))
- gram_norm: float32 [128, 128], replicated
- gram_rayleigh: float32 [128, 128], replicated
Inputs may be any that keep to these rules, and one draw needn't show every extreme that they name: `tile_rows`: let G = 16. Tiles k in [d * 8, (d + 1) * 8) lie on the device d = r * 32 + c; with p = c % G, that device's tiles have block rows in [max(r, p) * 12, (max(r, p) + 1) * 12) and block columns in [min(r, p) * 12, (min(r, p) + 1) * 12); where r equals p the block row is at least the block column. No position occurs twice. `tile_cols`: the block columns of the tiles described with tile_rows.
All inputs are finite; a program needn't handle non-finite values.
Results may differ from a plain program's by a relative error of at most 0.0039.
Values may be sent and summed in bfloat16 or wider, within the bound.
A program may use at most 64 MiB of HBM per device.

v0:
```python
import jax
import jax.numpy as jnp
from jax import lax
from jax.sharding import PartitionSpec as P

TS = 256
V = 128


def broadcast(array, axis, root):
    mine = lax.axis_index(axis) == root
    return lax.psum(jnp.where(mine, array, jnp.zeros_like(array)), axis)


def apply_group(own_group, tiles, tile_rows, tile_cols):
    groups = lax.axis_size("row")
    row_index = lax.axis_index("row")
    col_index = lax.axis_index("col")
    partner = col_index % groups
    lower_pair = partner <= row_index
    owner = partner == row_index
    nblocks = own_group.shape[0] // TS
    high_group = jnp.where(lower_pair, row_index, partner)
    low_group = jnp.where(lower_pair, partner, row_index)
    local_rows = tile_rows - high_group * nblocks
    local_cols = tile_cols - low_group * nblocks
    partner_group = broadcast(own_group, "row", partner)
    own_blocks = own_group.reshape(nblocks, TS, V)
    partner_blocks = partner_group.reshape(nblocks, TS, V)
    row_source = jnp.where(lower_pair, own_blocks, partner_blocks)
    col_source = jnp.where(lower_pair, partner_blocks, own_blocks)
    col_taken = jnp.take(col_source, local_cols, axis=0)
    row_taken = jnp.take(row_source, local_rows, axis=0)
    forward_part = jnp.einsum("kab,kbv->kav", tiles, col_taken, preferred_element_type=jnp.float32)
    backward_part = jnp.einsum("kba,kbv->kav", tiles, row_taken, preferred_element_type=jnp.float32)
    count = tiles.shape[0]
    block_ids = jnp.arange(nblocks, dtype=jnp.int32)[:, None]
    select_rows = (local_rows[None, :] == block_ids).astype(jnp.float32)
    select_cols = (local_cols[None, :] == block_ids).astype(jnp.float32)
    forward_sum = jnp.dot(
        select_rows, forward_part.reshape(count, TS * V), precision=lax.Precision.HIGHEST
    )
    backward_sum = jnp.dot(
        select_cols, backward_part.reshape(count, TS * V), precision=lax.Precision.HIGHEST
    )
    own_part = jnp.where(lower_pair, forward_sum, backward_sum)
    partner_part = jnp.where(lower_pair, backward_sum, forward_sum)
    total_rows = nblocks * TS
    extra_term = None
    summed = lax.psum(partner_part, "row")
    combined = own_part + jnp.where(owner, summed, jnp.zeros_like(summed))
    share = lax.psum_scatter(
        combined.reshape(total_rows, V), "col", scatter_dimension=0, tiled=True
    )
    return share.astype(jnp.bfloat16)


def gram_local(left, right):
    return lax.dot_general(
        left, right, (((0,), (0,)), ((), ())), preferred_element_type=jnp.float32
    )


def body(vectors, tiles, tile_rows, tile_cols):
    total_rows = vectors.shape[0] * lax.axis_size("row")
    applied = apply_group(vectors, tiles, tile_rows, tile_cols)
    norm_local = gram_local(applied, applied)
    gram_norm = lax.psum(norm_local, ("row", "col")) / total_rows
    applied_group = lax.all_gather(applied, "col", axis=0, tiled=True)
    applied_twice = apply_group(applied_group, tiles, tile_rows, tile_cols)
    rayleigh_local = gram_local(applied, applied_twice)
    gram_rayleigh = lax.psum(rayleigh_local, ("row", "col")) / total_rows
    return (applied, applied_twice, gram_norm, gram_rayleigh)


def solution(mesh):
    placed = (P("row", None), P(("row", "col"), None, None), P(("row", "col")), P(("row", "col")))
    return jax.shard_map(
        body,
        mesh=mesh,
        in_specs=placed,
        out_specs=(P(("row", "col"), None), P(("row", "col"), None), P(), P()),
        check_vma=False,
    )
```

profile of v0, /device:TPU:1, one launch (start us, length us, event | category | flops | bytes accessed | tf_op | source)
XLA Modules:
  0.0 1817.7 jit_solution(3547916854228819878)
XLA Ops:
  7.2 0.0 all-reduce.7.cloned.1.call-start
  7.3 1.0 broadcast_select_fusion.3
  8.3 0.0 all-reduce.7.cloned.1.call-update
  8.3 0.0 all-reduce.9.cloned.1.call-start
  8.5 207.6 %all-reduce.7.cloned.1.call-done = bf16[3072,128]{1,0:T(8,128)(2,1)} async-done(((bf16[3072,128]{1,0:T(8,128)(2,1)}), bf16[3072,128]{1,0:T(8,128)(2,1)}) %all-reduce.7.cloned.1.call-update) | async-done | bytes 786448 | tf_op jit(solution)/shard_map/psum | solution.py:12
  216.1 2.2 broadcast_select_fusion.7
  218.3 0.6 gather_fusion
  218.9 0.7 convolution_bitcast_fusion.3
  219.6 1.3 copy.9
  221.0 2.6 fusion.9
  223.6 2.5 gather_fusion.1
  226.2 2.4 convolution_bitcast_fusion.2
  228.6 2.5 copy.11
  231.1 4.6 broadcast_select_fusion.1
  235.8 0.0 all-reduce.9.cloned.1.call-update
  235.8 0.0 reduce-scatter.3.cloned.1.call-start
  235.8 268.1 %all-reduce.9.cloned.1.call-done = f32[12,32768]{1,0:T(8,128)} async-done(((f32[12,32768]{1,0:T(8,128)}), f32[12,32768]{1,0:T(8,128)}) %all-reduce.9.cloned.1.call-update) | async-done | bytes 1572880 | tf_op jit(solution)/shard_map/psum | solution.py:50
  503.9 3.2 select_add_fusion.1
  507.1 2.6 reshape.47
  509.7 0.0 reduce-scatter.3.cloned.1.call-update
  509.8 0.0 all-reduce.11.cloned.1.call-start
  509.8 152.8 %reduce-scatter.3.cloned.1.call-done = f32[96,128]{1,0:T(8,128)} async-done(((f32[3072,128]{1,0:T(8,128)}), f32[96,128]{1,0:T(8,128)}) %reduce-scatter.3.cloned.1.call-update) | async-done | bytes 49168 | tf_op jit(solution)/shard_map/reduce_scatter | solution.py:52
  662.6 0.8 convert_element_type.4
  663.4 44.8 %all_gather.3 = bf16[3072,128]{1,0:T(8,128)(2,1)S(1)} all-gather(bf16[96,128]{1,0:T(8,128)(2,1)S(1)} %convert_element_type.4), channel_id=1, replica_groups=mesh['row'=16,'col'=32] {'col'}, dimensions={0}, use_global_device_ids=true | all-gather | bytes 811008 | tf_op jit(solution)/shard_map/all_gather | solution.py:69
  708.1 1.0 broadcast_select_fusion.2
  709.1 0.0 all-reduce.13.cloned.1.call-start
  709.2 196.8 %all-reduce.11.cloned.1.call-done = bf16[3072,128]{1,0:T(8,128)(2,1)} async-done(((bf16[3072,128]{1,0:T(8,128)(2,1)}), bf16[3072,128]{1,0:T(8,128)(2,1)}) %all-reduce.11.cloned.1.call-update) | async-done | bytes 786448 | tf_op jit(solution)/shard_map/psum | solution.py:12
  906.0 2.2 broadcast_select_fusion.5
  908.2 0.6 gather_fusion.2
  908.8 0.7 convolution_bitcast_fusion.1
  909.6 1.3 copy.13
  910.9 2.6 fusion.3
  913.5 2.5 gather_fusion.3
  916.1 2.4 convolution_bitcast_fusion
  918.5 2.5 copy.15
  921.0 4.6 broadcast_select_fusion
  925.7 0.0 all-reduce.13.cloned.1.call-update
  925.7 0.0 reduce-scatter.5.cloned.1.call-start
  925.7 268.8 %all-reduce.13.cloned.1.call-done = f32[12,32768]{1,0:T(8,128)} async-done(((f32[12,32768]{1,0:T(8,128)}), f32[12,32768]{1,0:T(8,128)}) %all-reduce.13.cloned.1.call-update) | async-done | bytes 1572880 | tf_op jit(solution)/shard_map/psum | solution.py:50
  1194.5 3.2 select_add_fusion
  1197.7 2.6 reshape.50
  1200.4 0.0 all-reduce.15.cloned.1.call-start
  1200.5 0.8 fusion.32
  1201.3 152.0 %reduce-scatter.5.cloned.1.call-done = f32[96,128]{1,0:T(8,128)} async-done(((f32[3072,128]{1,0:T(8,128)}), f32[96,128]{1,0:T(8,128)}) %reduce-scatter.5.cloned.1.call-update) | async-done | bytes 49168 | tf_op jit(solution)/shard_map/reduce_scatter | solution.py:52
  1353.2 0.8 convert_element_type.5
  1354.0 0.8 fusion.33
  1354.9 454.5 %all-reduce.15.cloned.1.call-done = (f32[128,128]{1,0:T(8,128)}, f32[128,128]{1,0:T(8,128)}) async-done(((f32[128,128]{1,0:T(8,128)}, f32[128,128]{1,0:T(8,128)}), (f32[128,128]{1,0:T(8,128)}, f32[128,128]{1,0:T(8,128)})) %all-reduce.15.cloned.1.call-update) | async-done | bytes 131088 | tf_op jit(solution)/shard_map/psum | solution.py:68
  1809.4 1.5 broadcast_multiply_fusion
  (21 shorter events, 0.1 us)
Async XLA Ops:
  7.2 211.7 %copy-start = (bf16[8,256,256]{2,1,0:T(8,128)(2,1)S(1)}, bf16[8,256,256]{2,1,0:T(8,128)(2,1)}, u32[]{:S(2)}) copy-start(bf16[8,256,256]{2,1,0:T(8,128)(2,1)} %param.7) | copy-start | bytes 3145732
  7.2 208.9 %copy-start.1 = (bf16[3072,128]{1,0:T(8,128)(2,1)S(1)}, bf16[3072,128]{1,0:T(8,128)(2,1)}, u32[]{:S(2)}) copy-start(bf16[3072,128]{1,0:T(8,128)(2,1)} %param.6) | copy-start | bytes 2359300
  7.2 1.2 copy-start.4
  7.2 1.2 copy-start.5
  7.2 208.9 %all-reduce.7.cloned.1.call-start = ((), (), s32[]{:S(2)}) async-start(), calls=%async_computation.2 | async-start | bytes 1572864 | tf_op jit(solution)/shard_map/psum | solution.py:12
  8.3 495.6 %all-reduce.9.cloned.1.call-start = ((), (), s32[]{:S(2)}) async-start(), calls=%async_computation.3 | async-start | bytes 4194304 | tf_op jit(solution)/shard_map/psum | solution.py:50
  235.8 426.8 %reduce-scatter.3.cloned.1.call-start = ((), (), s32[]{:S(2)}) async-start(), calls=%async_computation.4 | async-start | bytes 1622016 | tf_op jit(solution)/shard_map/reduce_scatter | solution.py:52
  509.8 396.2 %all-reduce.11.cloned.1.call-start = ((), (), s32[]{:S(2)}) async-start(), calls=%async_computation.5 | async-start | bytes 1572864 | tf_op jit(solution)/shard_map/psum | solution.py:12
  663.4 690.7 %copy-start.2 = (bf16[96,128]{1,0:T(8,128)(2,1)}, bf16[96,128]{1,0:T(8,128)(2,1)S(1)}, u32[]{:S(2)}) copy-start(bf16[96,128]{1,0:T(8,128)(2,1)S(1)} %convert_element_type.4) | copy-start | bytes 73732
  709.1 485.4 %all-reduce.13.cloned.1.call-start = ((), (), s32[]{:S(2)}) async-start(), calls=%async_computation.6 | async-start | bytes 4194304 | tf_op jit(solution)/shard_map/psum | solution.py:50
  925.7 427.5 %reduce-scatter.5.cloned.1.call-start = ((), (), s32[]{:S(2)}) async-start(), calls=%async_computation.7 | async-start | bytes 1622016 | tf_op jit(solution)/shard_map/reduce_scatter | solution.py:52
  1200.4 608.9 %all-reduce.15.cloned.1.call-start = ((), (), s32[]{:S(2)}) async-start(), calls=%async_computation.8 | async-start | bytes 262144 | tf_op jit(solution)/shard_map/psum | solution.py:68
  1354.0 456.8 %copy-start.3 = (bf16[96,128]{1,0:T(8,128)(2,1)}, bf16[96,128]{1,0:T(8,128)(2,1)S(1)}, u32[]{:S(2)}) copy-start(bf16[96,128]{1,0:T(8,128)(2,1)S(1)} %convert_element_type.5) | copy-start | bytes 73732
Sparse Core Ops, SparseCore 0:
  11.0 205.0 all-reduce.6
  235.9 267.9 all-reduce.8
  509.9 152.6 reduce-scatter.2
  709.3 196.6 all-reduce.10
  925.8 268.6 all-reduce.12
  1200.5 152.6 reduce-scatter.4
  1359.4 449.9 all-reduce.14
where the time goes:
time: 1820 us
  waiting for transfers between devices  1700 us (93%)
  blocking collectives  44.8 us (2%)
  matrix products  22.5 us (1%)
  local copies, waits for them, and re-layouts  19.4 us (1%)
    psum x2, waiting for transfers between devices, apply_group(): summed = lax.psum(partner_part, 'row')  537 us
    psum x1, waiting for transfers between devices, body(): gram_norm = lax.psum(norm_local, ('row', 'col')) / total_rows  454 us
    psum x2, waiting for transfers between devices, broadcast(): return lax.psum(jnp.where(mine, array, jnp.zeros_like(array)), axis)  404 us
    reduce_scatter x2, waiting for transfers between devices, apply_group(): lax.psum_scatter(combined.reshape(total_rows, V), 'col', scatter_dimensio...  305 us
    all_gather x1, blocking collectives, body(): applied_group = lax.all_gather(applied, 'col', axis=0, tiled=True)  44.8 us
  transfers between devices with their start and end apart: 7, of which 7 were waited for; matrix products, arithmetic and copies ran while one was open for 0% of the time, Pallas kernels for 0%

commit v1 on v0

v1 whole, which is shorter than its diff:
```python
import jax
import jax.numpy as jnp
from jax import lax
from jax.experimental import pallas as pl
from jax.experimental.pallas import tpu as pltpu
from jax.sharding import PartitionSpec as P

MESH = pl.DeviceIdType.MESH
BF = jnp.bfloat16
F32 = jnp.float32
TS = 256
V = 128
NB = 12
G = 16
NCOL = 32
K = 8
GROUP = NB * TS
CH = GROUP // NCOL
QU = GROUP // 4
NROWS = GROUP * G

ZIN, YIN, YRS, ZOUT, OOUT, OIN, G1, G2, G3 = range(9)


def loop(n, body):
    def step(i, carry):
        body(i)
        return carry

    lax.fori_loop(0, n, step, 0)


def kernel(
    vec, tiles, trows, tcols, out1, out2, gn, gr,
    tt, up0, up1, uo, prod, pb, ob, yr, zs, zr, orr, ach, gs, gr1, gp, gr2, gf, ga,
    ssem, rsem,
):
    up = (up0, up1)
    r = lax.axis_index("row")
    c = lax.axis_index("col")
    y, zh = r // 4, r % 4
    zl = c // 8
    p = c % G
    is_high = p <= r
    self_z = jnp.logical_and(p == r, y == zl)

    def wait_bytes(ref, sem):
        pltpu.make_async_copy(ref, ref, sem).wait()

    def z_group(i):
        return 4 * zl + i // 2, r + G * (i % 2)

    def z_owner(i):
        return p, 8 * y + i

    barrier = pltpu.get_barrier_semaphore()

    def greet(row, col):
        pl.semaphore_signal(barrier, inc=1, device_id=(row, col), device_id_type=MESH)

    def greet_other(row, col):
        @pl.when(jnp.logical_or(row != r, col != c))
        def _():
            greet(row, col)

    loop(NCOL - 1, lambda i: greet(r, (c + i + 1) % NCOL))
    loop(G - 1, lambda i: greet((r + i + 1) % G, c))
    loop(8, lambda i: greet_other(*z_group(i)))
    loop(8, lambda i: greet_other(*z_owner(i)))

    straight = jnp.where(is_high, 0, 1)

    def turn(k):
        t = tiles[k]
        tt[straight, k] = t
        tt[1 - straight, k] = t.T

    loop(K, turn)

    def within(block):
        return jnp.minimum(jnp.maximum(block, 0), NB - 1)

    def own_id(k):
        return within(jnp.where(is_high, trows[k], tcols[k]) - r * NB)

    def par_id(k):
        return within(jnp.where(is_high, tcols[k], trows[k]) - p * NB)

    pl.semaphore_wait(barrier, NCOL - 1 + G - 1 + 16 - 2 * jnp.where(self_z, 1, 0))

    def send(src, dst, a, stage, row, col):
        pltpu.make_async_remote_copy(
            src_ref=src,
            dst_ref=dst,
            send_sem=ssem.at[a, stage],
            recv_sem=rsem.at[a, stage],
            device_id=(row, col),
            device_id_type=MESH,
        ).start()

    def send_or_copy(src, dst, a, stage, row, col):
        same = jnp.logical_and(row == r, col == c)

        @pl.when(same)
        def _():
            pltpu.make_async_copy(src, dst, rsem.at[a, stage]).start()

        @pl.when(jnp.logical_not(same))
        def _():
            send(src, dst, a, stage, row, col)

    def rows(ref, start, count):
        return ref.at[pl.ds(pl.multiple_of(start, 32), count)]

    def z_in(a, src):
        def body(i):
            send_or_copy(src, rows(up[a], c * CH, CH), a, ZIN, *z_group(i))

        loop(8, body)

    def y_in(a):
        wait_bytes(up[a].at[pl.ds(0, QU)], rsem.at[a, ZIN])
        part = rows(up[a], y * QU, QU)

        def body(i):
            send(part, part, a, YIN, 4 * ((y + i + 1) % 4) + zh, c)

        loop(3, body)

    def own_in(a):
        def body(i):
            send(ach, rows(uo, c * CH, CH), a, OIN, r, (c + i + 1) % NCOL)

        loop(NCOL - 1, body)

    def one_if_same(left, right):
        gap = left - right
        return (1 - jnp.minimum(gap * gap, 1)).astype(F32)

    def products(side, ids_from, source, ids_to, target):
        def one(k):
            block = source[pl.ds(ids_from(k) * TS, TS), :]
            prod[k] = jnp.dot(tt[side, k], block, preferred_element_type=F32)

        loop(K, one)

        def gather(b):
            weights = [one_if_same(ids_to(k), b) for k in range(K)]
            for q in range(4):
                piece = pl.ds(64 * q, 64)
                acc = prod[0, piece, :] * weights[0]
                for k in range(1, K):
                    acc = acc + prod[k, piece, :] * weights[k]
                target[pl.ds(pl.multiple_of(b * TS + 64 * q, 64), 64), :] = acc.astype(BF)

        loop(NB, gather)

    def y_out(a):
        def body(i):
            to = (y + i + 1) % 4
            send(rows(pb.at[a], to * QU, QU), yr.at[a, i], a, YRS, 4 * to + zh, c)

        loop(3, body)

    def z_out(a):
        wait_bytes(yr.at[a], rsem.at[a, YRS])

        def add(j):
            at = pl.multiple_of(j * CH, CH)
            acc = pb[a, pl.ds(pl.multiple_of(y * QU + j * CH, CH), CH), :].astype(F32)
            for i in range(3):
                acc = acc + yr[a, i, pl.ds(at, CH), :].astype(F32)
            zs[a, pl.ds(at, CH), :] = acc.astype(BF)

        loop(8, add)
        slot = zh * 2 + c // G

        def body(i):
            send_or_copy(rows(zs.at[a], i * CH, CH), zr.at[a, slot], a, ZOUT, *z_owner(i))

        loop(8, body)

    def own_out(a):
        def body(i):
            to = (c + i + 1) % NCOL
            send(rows(ob.at[a], to * CH, CH), orr.at[a, i], a, OOUT, r, to)

        loop(NCOL - 1, body)

    def total(a):
        wait_bytes(orr.at[a], rsem.at[a, OOUT])
        wait_bytes(zr.at[a], rsem.at[a, ZOUT])
        acc = ob[a, pl.ds(pl.multiple_of(c * CH, CH), CH), :].astype(F32)
        acc = lax.fori_loop(0, NCOL - 1, lambda i, s: s + orr[a, i].astype(F32), acc)
        acc = lax.fori_loop(0, 8, lambda i, s: s + zr[a, i].astype(F32), acc)
        return acc.astype(BF)

    def inner(left, right):
        return lax.dot_general(left, right, (((0,), (0,)), ((), ())), preferred_element_type=F32)

    z_in(0, rows(vec, c * CH, CH))
    products(1, own_id, vec, par_id, pb.at[0])
    y_out(0)
    y_in(0)
    z_out(0)
    wait_bytes(up[0].at[pl.ds(0, 3 * QU)], rsem.at[0, YIN])
    products(0, par_id, up[0], own_id, ob.at[0])
    own_out(0)
    first = total(0)
    ach[...] = first
    out1[...] = first

    z_in(1, ach)
    own_in(1)
    uo[pl.ds(pl.multiple_of(c * CH, CH), CH), :] = first
    gs[pl.ds(0, V), :] = inner(first, first)
    y_in(1)
    wait_bytes(uo.at[pl.ds(0, GROUP - CH)], rsem.at[1, OIN])
    products(1, own_id, uo, par_id, pb.at[1])
    y_out(1)
    wait_bytes(up[1].at[pl.ds(0, 3 * QU)], rsem.at[1, YIN])
    products(0, par_id, up[1], own_id, ob.at[1])
    own_out(1)

    gs[pl.ds(V, V), :] = inner(uo[...], ob[1]) + inner(up[1][...], pb[1])

    def gram_out(i):
        to = (c + i + 1) % NCOL
        send(gs.at[pl.ds(pl.multiple_of(to * 8, 8), 8)], gr1.at[i], 1, G1, r, to)

    loop(NCOL - 1, gram_out)
    z_out(1)

    wait_bytes(gr1, rsem.at[1, G1])
    acc = gs[pl.ds(pl.multiple_of(c * 8, 8), 8), :]
    gp[...] = lax.fori_loop(0, NCOL - 1, lambda i, s: s + gr1[i], acc)
    loop(G - 1, lambda i: send(gp, gr2.at[i], 1, G2, (r + i + 1) % G, c))
    second = total(1)
    out2[...] = second

    wait_bytes(gr2, rsem.at[1, G2])
    acc = lax.fori_loop(0, G - 1, lambda i, s: s + gr2[i], gp[...])
    gf[...] = acc
    mine = pl.ds(pl.multiple_of(c * 8, 8), 8)
    loop(NCOL - 1, lambda i: send(gf, ga.at[mine], 1, G3, r, (c + i + 1) % NCOL))
    ga[mine, :] = acc
    wait_bytes(ga.at[pl.ds(0, 2 * V - 8)], rsem.at[1, G3])
    gn[...] = ga[pl.ds(0, V), :] / NROWS
    gr[...] = ga[pl.ds(V, V), :] / NROWS

    for a in range(2):
        @pl.when(self_z)
        def _():
            wait_bytes(up[a].at[pl.ds(0, 7 * CH)], ssem.at[a, ZIN])
            wait_bytes(up[a].at[pl.ds(0, 7 * CH)], ssem.at[a, ZOUT])

        @pl.when(jnp.logical_not(self_z))
        def _():
            wait_bytes(up[a].at[pl.ds(0, 8 * CH)], ssem.at[a, ZIN])
            wait_bytes(up[a].at[pl.ds(0, 8 * CH)], ssem.at[a, ZOUT])

        wait_bytes(up[a].at[pl.ds(0, 3 * QU)], ssem.at[a, YIN])
        wait_bytes(yr.at[a], ssem.at[a, YRS])
        wait_bytes(orr.at[a], ssem.at[a, OOUT])
    wait_bytes(orr.at[1], ssem.at[1, OIN])
    wait_bytes(gr1, ssem.at[1, G1])
    wait_bytes(gr2, ssem.at[1, G2])
    wait_bytes(gr1, ssem.at[1, G3])


def body(vectors, tiles, tile_rows, tile_cols):
    vmem = pl.BlockSpec(memory_space=pltpu.VMEM)
    smem = pl.BlockSpec(memory_space=pltpu.SMEM)
    return pl.pallas_call(
        kernel,
        out_shape=(
            jax.ShapeDtypeStruct((CH, V), BF),
            jax.ShapeDtypeStruct((CH, V), BF),
            jax.ShapeDtypeStruct((V, V), F32),
            jax.ShapeDtypeStruct((V, V), F32),
        ),
        in_specs=[vmem, vmem, smem, smem],
        out_specs=(vmem,) * 4,
        scratch_shapes=[
            pltpu.VMEM((2, K, TS, TS), BF),
            pltpu.VMEM((GROUP, V), BF),
            pltpu.VMEM((GROUP, V), BF),
            pltpu.VMEM((GROUP, V), BF),
            pltpu.VMEM((K, TS, V), F32),
            pltpu.VMEM((2, GROUP, V), BF),
            pltpu.VMEM((2, GROUP, V), BF),
            pltpu.VMEM((2, 3, QU, V), BF),
            pltpu.VMEM((2, QU, V), BF),
            pltpu.VMEM((2, 8, CH, V), BF),
            pltpu.VMEM((2, NCOL - 1, CH, V), BF),
            pltpu.VMEM((CH, V), BF),
            pltpu.VMEM((2 * V, V), F32),
            pltpu.VMEM((NCOL - 1, 8, V), F32),
            pltpu.VMEM((8, V), F32),
            pltpu.VMEM((G - 1, 8, V), F32),
            pltpu.VMEM((8, V), F32),
            pltpu.VMEM((2 * V, V), F32),
            pltpu.SemaphoreType.DMA((2, 9)),
            pltpu.SemaphoreType.DMA((2, 9)),
        ],
        compiler_params=pltpu.CompilerParams(
            collective_id=0, has_side_effects=True, vmem_limit_bytes=40 * 2**20
        ),
    )(vectors, tiles, tile_rows, tile_cols)


def solution(mesh):
    placed = (P("row", None), P(("row", "col"), None, None), P(("row", "col")), P(("row", "col")))
    return jax.shard_map(
        body,
        mesh=mesh,
        in_specs=placed,
        out_specs=(P(("row", "col"), None), P(("row", "col"), None), P(), P()),
        check_vma=False,
    )
```

time: 1820 us -> 179 us (0.10)
  waiting for transfers between devices: 1700 us -> 0 us
  Pallas kernels: 0 us -> 172 us
  blocking collectives: 44.8 us -> 0 us
  matrix products: 22.5 us -> 0 us
    psum x5 -> x0, waiting for transfers between devices: 1400 us -> none  [the longest x2 537 us: apply_group(): summed = lax.psum(partner_part, 'row')]
    reduce_scatter x2 -> x0, waiting for transfers between devices: 305 us -> none  [apply_group(): lax.psum_scatter(combined.reshape(total_rows, V), 'col', scatter_dimensio...]
    pallas_call x0 -> x1, Pallas kernels: none -> 172 us  [body(): pl.pallas_call(kernel, out_shape=(jax.ShapeDtypeStruct((CH, V), BF), jax....]
    all_gather x1 -> x0, blocking collectives: 44.8 us -> none  [body(): applied_group = lax.all_gather(applied, 'col', axis=0, tiled=True)]
    dot_general x10 -> x0, matrix products: 22.5 us -> none  [the longest x2 9.26 us: apply_group(): jnp.dot(select_cols, backward_part.reshape(count, TS * V), precision=lax....]
  transfers between devices with their start and end apart: 7 -> 0, of which waited for: 7 -> 0; matrix products, arithmetic and copies ran while one was open for 0% -> 0% of each run, Pallas kernels for 0% -> 0%
where the time goes in v1:
time: 179 us
  Pallas kernels  172 us (96%)
  local copies, waits for them, and re-layouts  6.14 us (3%)
    pallas_call x1, Pallas kernels, body(): pl.pallas_call(kernel, out_shape=(jax.ShapeDtypeStruct((CH, V), BF), jax....  172 us
    unnamed x12, local copies, waits for them, and re-layouts  6.14 us

profile of v1, /device:TPU:1, one launch (start us, length us, event | category | flops | bytes accessed | tf_op | source)
XLA Modules:
  0.0 178.7 jit_solution(13661772557841310399)
XLA Ops:
  0.6 0.0 copy-start
  0.6 1.2 copy-done
  1.9 0.0 copy-start.1
  1.9 1.1 copy-done.1
  3.0 0.0 copy-start.2
  3.0 0.7 copy-done.2
  3.6 0.0 copy-start.3
  3.6 0.7 copy-done.3
  4.3 171.9 %shard_map.75 = (bf16[96,128]{1,0:T(8,128)(2,1)S(1)}, bf16[96,128]{1,0:T(8,128)(2,1)S(1)}, f32[128,128]{1,0:T(8,128)S(1)}, f32[128,128]{1,0:T(8,128)S(1)}) custom-call(bf16[3072,128]{1,0:T(8,128)(2,1)S(1)} %copy-done.1, bf16[8,256,256]{2,1,0:T(8,128)(2,1)S(1)} %copy-done, s32[8]{0:T(128)S(1)} %copy-done.2, s32[8]{0:T(128)S(1)} %copy-done.3), custom_call_target="tpu_custom_call" | custom-call | tf_op jit(solution)/shard_map/pallas_call | solution.py:274
  176.2 0.6 copy.12
  176.8 0.6 copy.13
  177.4 0.6 copy.14
  178.0 0.6 copy.15
Async XLA Ops:
  0.6 1.2 copy-start
  1.9 1.1 copy-start.1
  3.0 0.7 copy-start.2
  3.6 0.7 copy-start.3

commit v2 on v1

v2 whole, which is shorter than its diff:
```python
import jax
import jax.numpy as jnp
from jax import lax
from jax.experimental import pallas as pl
from jax.experimental.pallas import tpu as pltpu
from jax.sharding import PartitionSpec as P

MESH = pl.DeviceIdType.MESH
BF = jnp.bfloat16
F32 = jnp.float32
TS = 256
V = 128
NB = 12
G = 16
NCOL = 32
K = 8
GROUP = NB * TS
CH = GROUP // NCOL
QU = GROUP // 4
NROWS = GROUP * G

ZIN, YIN, YRS, ZOUT, OZ, OX, XRS, OOUT, G1, G2, G3 = range(11)
NSTAGE = 11


def loop(n, body):
    def step(i, carry):
        body(i)
        return carry

    lax.fori_loop(0, n, step, 0)


def kernel(
    vec_in, tiles_in, trows, tcols, out1, out2, gn, gr,
    vec, tiles, tt, up0, up1, uo, prod, pb, ob, yr, xr, zs, zr, osum, orr, ach,
    gs, gr1, gp, gr2, gf, ga, ssem, rsem, lsem,
):
    up = (up0, up1)
    r = lax.axis_index("row")
    c = lax.axis_index("col")
    y, zh = r // 4, r % 4
    zl, xk = c // 8, c % 8
    x, k = xk // 2, c % 2
    x1 = x + 1 - 2 * (x % 2)
    par = zl % 2
    p = c % G
    p1 = 8 * par + 2 * x1 + k
    is_high = p <= r
    to_xk = 2 * ((x + 2 * (y // 2)) % 4) + y % 2
    self_z = jnp.logical_and(p == r, y == zl)
    self_out = jnp.logical_and(jnp.logical_or(p == r, p1 == r), to_xk == xk)

    load_vec = pltpu.make_async_copy(vec_in, vec, lsem.at[0])
    load_tiles = pltpu.make_async_copy(tiles_in, tiles, lsem.at[1])
    load_vec.start()
    load_tiles.start()

    def wait_bytes(ref, sem):
        pltpu.make_async_copy(ref, ref, sem).wait()

    def z_group(i):
        return 4 * zl + (zh + 2 + i // 2) % 4, r + G * (i % 2)

    def z_owner(i):
        return p, 8 * y + i

    def out_owner(q, e):
        return (p if e == 0 else p1), 8 * q + to_xk

    rx, rk, rpar = (r // 2) % 4, r % 2, r // 8
    flip = (x % 2 + rx % 2) % 2
    from_y = 2 * ((x // 2 + rx // 2) % 2) + k
    from_x = rx + flip * (1 - 2 * (rx % 2))

    def out_source(i):
        return 4 * from_y + i // 2, 8 * (rpar + 2 * (i % 2)) + 2 * from_x + rk

    def pair_mate(j):
        return 4 * j + zh, 8 * zl + 2 * x1 + k

    barrier = pltpu.get_barrier_semaphore()

    def greet(row, col):
        pl.semaphore_signal(barrier, inc=1, device_id=(row, col), device_id_type=MESH)

    def greet_other(row, col):
        @pl.when(jnp.logical_or(row != r, col != c))
        def _():
            greet(row, col)

    loop(8, lambda i: greet_other(*z_group(i)))
    loop(8, lambda i: greet_other(*z_owner(i)))
    loop(4, lambda q: greet_other(*out_owner(q, 0)))
    loop(4, lambda q: greet_other(*out_owner(q, 1)))
    loop(8, lambda i: greet_other(*out_source(i)))
    loop(G - 1, lambda i: greet((r + i + 1) % G, c))
    loop(4, lambda j: greet(*pair_mate(j)))
    loop(NCOL - 1, lambda i: greet(r, (c + i + 1) % NCOL))

    straight = jnp.where(is_high, 0, 1)
    load_vec.wait()
    load_tiles.wait()

    def turn(k):
        t = tiles[k]
        tt[straight, k] = t
        tt[1 - straight, k] = t.T

    loop(K, turn)

    def within(block):
        return jnp.minimum(jnp.maximum(block, 0), NB - 1)

    def own_id(k):
        return within(jnp.where(is_high, trows[k], tcols[k]) - r * NB)

    def par_id(k):
        return within(jnp.where(is_high, tcols[k], trows[k]) - p * NB)

    def send(src, dst, a, stage, sub, row, col):
        pltpu.make_async_remote_copy(
            src_ref=src,
            dst_ref=dst,
            send_sem=ssem.at[a, stage],
            recv_sem=rsem.at[a, stage, sub],
            device_id=(row, col),
            device_id_type=MESH,
        ).start()

    def send_or_copy(src, dst, a, stage, sub, row, col):
        same = jnp.logical_and(row == r, col == c)

        @pl.when(same)
        def _():
            pltpu.make_async_copy(src, dst, rsem.at[a, stage, sub]).start()

        @pl.when(jnp.logical_not(same))
        def _():
            send(src, dst, a, stage, sub, row, col)

    def chunk(ref, i):
        return ref.at[pl.ds(pl.multiple_of(i * CH, CH), CH)]

    def read(ref, a, i):
        return ref[a, pl.ds(pl.multiple_of(i * CH, CH), CH), :].astype(F32)

    def z_in(a, src):
        loop(8, lambda i: send_or_copy(src, chunk(up[a], c), a, ZIN, xk, *z_group(i)))

    def y_in(a):
        def forward(i):
            part = chunk(up[a], 8 * y + i)
            wait_bytes(part, rsem.at[a, ZIN, i])
            loop(3, lambda j: send(part, part, a, YIN, 0, 4 * ((y + j + 1) % 4) + zh, c))

        loop(8, forward)

    def to_mates(src, where):
        loop(7, lambda i: send(src, chunk(uo, where), 1, OX, 0, r, 8 * zl + (xk + i + 1) % 8))

    def own_in():
        loop(3, lambda i: send(ach, chunk(uo, c), 1, OZ, i, r, 8 * ((zl + i + 1) % 4) + xk))
        to_mates(ach, c)

        def forward(i):
            cc = 8 * ((zl + 3 - i) % 4) + xk
            part = chunk(uo, cc)
            wait_bytes(part, rsem.at[1, OZ, i])
            to_mates(part, cc)

        loop(3, forward)

    def one_if_same(left, right):
        gap = left - right
        return (1 - jnp.minimum(gap * gap, 1)).astype(F32)

    def multiply(side, ids_from, source):
        def one(k):
            block = source[pl.ds(ids_from(k) * TS, TS), :]
            prod[k] = jnp.dot(tt[side, k], block, preferred_element_type=F32)

        loop(K, one)

    def gather(ids_to, target, a, q):
        def block(i):
            b = 3 * q + i
            weights = [one_if_same(ids_to(k), b) for k in range(K)]
            for s in range(4):
                piece = pl.ds(64 * s, 64)
                acc = prod[0, piece, :] * weights[0]
                for k in range(1, K):
                    acc = acc + prod[k, piece, :] * weights[k]
                target[a, pl.ds(pl.multiple_of(b * TS + 64 * s, 64), 64), :] = acc.astype(BF)

        loop(3, block)

    def y_out(a, q):
        def mate(i):
            j = (y + i + 1) % 4
            part = chunk(pb.at[a], 8 * q + 2 * ((x + 2 * (j // 2)) % 4) + j % 2)
            send(part, yr.at[a, q, i], a, YRS, q, 4 * j + zh, c)

        def pair(i):
            j = (y + i) % 4
            part = chunk(pb.at[a], 8 * q + 2 * ((x1 + 2 * (j // 2)) % 4) + j % 2)
            send(part, yr.at[a, q, 3 + i], a, YRS, q, *pair_mate(j))

        loop(4, pair)
        loop(3, mate)

    def z_out(a):
        slot = zh * 2 + c // G

        def step(q):
            wait_bytes(yr.at[a, q], rsem.at[a, YRS, q])
            acc = read(pb, a, 8 * q + to_xk)
            for i in range(3):
                acc = acc + yr[a, q, i].astype(F32)
            zs[a, q, 0] = acc.astype(BF)
            acc = yr[a, q, 3].astype(F32)
            for i in range(4, 7):
                acc = acc + yr[a, q, i].astype(F32)
            zs[a, q, 1] = acc.astype(BF)
            send_or_copy(zs.at[a, q, 0], zr.at[a, slot], a, ZOUT, 0, *out_owner(q, 0))
            send_or_copy(zs.at[a, q, 1], zr.at[a, slot], a, ZOUT, 0, *out_owner(q, 1))

        loop(4, step)

    def x_out(a, q):
        def mate(i):
            to = (xk + i + 1) % 8
            send(chunk(ob.at[a], 8 * q + to), xr.at[a, q, i], a, XRS, q, r, 8 * zl + to)

        loop(7, mate)

    def own_sum(a, q):
        wait_bytes(xr.at[a, q], rsem.at[a, XRS, q])
        acc = read(ob, a, 8 * q + xk)
        for i in range(7):
            acc = acc + xr[a, q, i].astype(F32)
        osum[a, q] = acc

    def own_out(a):
        def step(i):
            q = (zl + i + 1) % 4
            own_sum(a, q)
            send(osum.at[a, q], orr.at[a, i], a, OOUT, 0, r, 8 * q + xk)

        loop(3, step)
        own_sum(a, zl)

    def total(a):
        wait_bytes(orr.at[a], rsem.at[a, OOUT, 0])
        wait_bytes(zr.at[a], rsem.at[a, ZOUT, 0])
        acc = osum[a, zl]
        for i in range(3):
            acc = acc + orr[a, i]
        for i in range(8):
            acc = acc + zr[a, i].astype(F32)
        return acc.astype(BF)

    def inner(left, right):
        return lax.dot_general(left, right, (((0,), (0,)), ((), ())), preferred_element_type=F32)

    multiply(1, own_id, vec)
    loop(4, lambda q: gather(par_id, pb, 0, q))
    waits = NCOL - 1 + G - 1 + 4 + 32
    pl.semaphore_wait(
        barrier, waits - 2 * jnp.where(self_z, 1, 0) - 2 * jnp.where(self_out, 1, 0)
    )
    z_in(0, chunk(vec, c))
    loop(4, lambda q: y_out(0, q))
    z_out(0)
    y_in(0)
    wait_bytes(up[0].at[pl.ds(0, 3 * QU)], rsem.at[0, YIN, 0])
    multiply(0, par_id, up[0])

    def finish_own(a):
        def step(i):
            q = (zl + i + 1) % 4
            gather(own_id, ob, a, q)
            x_out(a, q)

        loop(4, step)

    finish_own(0)
    own_out(0)
    first = total(0)
    ach[...] = first
    out1[...] = first

    z_in(1, ach)
    own_in()
    uo[pl.ds(pl.multiple_of(c * CH, CH), CH), :] = first
    gs[pl.ds(0, V), :] = inner(first, first)
    wait_bytes(uo.at[pl.ds(0, 28 * CH)], rsem.at[1, OX, 0])
    multiply(1, own_id, uo)

    def partner_step(q):
        gather(par_id, pb, 1, q)
        y_out(1, q)

    loop(4, partner_step)
    y_in(1)
    z_out(1)
    wait_bytes(up[1].at[pl.ds(0, 3 * QU)], rsem.at[1, YIN, 0])
    multiply(0, par_id, up[1])
    finish_own(1)

    gs[pl.ds(V, V), :] = inner(uo[...], ob[1]) + inner(up[1][...], pb[1])

    def gram_out(i):
        to = (c + i + 1) % NCOL
        send(gs.at[pl.ds(pl.multiple_of(to * 8, 8), 8)], gr1.at[i], 1, G1, 0, r, to)

    loop(NCOL - 1, gram_out)
    own_out(1)

    wait_bytes(gr1, rsem.at[1, G1, 0])
    acc = gs[pl.ds(pl.multiple_of(c * 8, 8), 8), :]
    gp[...] = lax.fori_loop(0, NCOL - 1, lambda i, s: s + gr1[i], acc)
    loop(G - 1, lambda i: send(gp, gr2.at[i], 1, G2, 0, (r + i + 1) % G, c))
    second = total(1)
    out2[...] = second

    wait_bytes(gr2, rsem.at[1, G2, 0])
    acc = lax.fori_loop(0, G - 1, lambda i, s: s + gr2[i], gp[...])
    gf[...] = acc
    mine = pl.ds(pl.multiple_of(c * 8, 8), 8)
    loop(NCOL - 1, lambda i: send(gf, ga.at[mine], 1, G3, 0, r, (c + i + 1) % NCOL))
    ga[mine, :] = acc
    wait_bytes(ga.at[pl.ds(0, 2 * V - 8)], rsem.at[1, G3, 0])
    gn[...] = ga[pl.ds(0, V), :] / NROWS
    gr[...] = ga[pl.ds(V, V), :] / NROWS

    def sent(a, stage, less, chunks):
        @pl.when(less)
        def _():
            wait_bytes(up[a].at[pl.ds(0, (chunks - 1) * CH)], ssem.at[a, stage])

        @pl.when(jnp.logical_not(less))
        def _():
            wait_bytes(up[a].at[pl.ds(0, chunks * CH)], ssem.at[a, stage])

    for a in range(2):
        sent(a, ZIN, self_z, 8)
        sent(a, ZOUT, self_out, 8)
        wait_bytes(up[a].at[pl.ds(0, 24 * CH)], ssem.at[a, YIN])
        wait_bytes(yr.at[a], ssem.at[a, YRS])
        wait_bytes(xr.at[a], ssem.at[a, XRS])
        wait_bytes(orr.at[a], ssem.at[a, OOUT])
    wait_bytes(uo.at[pl.ds(0, 3 * CH)], ssem.at[1, OZ])
    wait_bytes(uo.at[pl.ds(0, 28 * CH)], ssem.at[1, OX])
    wait_bytes(gr1, ssem.at[1, G1])
    wait_bytes(gr2, ssem.at[1, G2])
    wait_bytes(gr1, ssem.at[1, G3])


def body(vectors, tiles, tile_rows, tile_cols):
    vmem = pl.BlockSpec(memory_space=pltpu.VMEM)
    smem = pl.BlockSpec(memory_space=pltpu.SMEM)
    hbm = pl.BlockSpec(memory_space=pltpu.HBM)
    return pl.pallas_call(
        kernel,
        out_shape=(
            jax.ShapeDtypeStruct((CH, V), BF),
            jax.ShapeDtypeStruct((CH, V), BF),
            jax.ShapeDtypeStruct((V, V), F32),
            jax.ShapeDtypeStruct((V, V), F32),
        ),
        in_specs=[hbm, hbm, smem, smem],
        out_specs=(vmem,) * 4,
        scratch_shapes=[
            pltpu.VMEM((GROUP, V), BF),
            pltpu.VMEM((K, TS, TS), BF),
            pltpu.VMEM((2, K, TS, TS), BF),
            pltpu.VMEM((GROUP, V), BF),
            pltpu.VMEM((GROUP, V), BF),
            pltpu.VMEM((GROUP, V), BF),
            pltpu.VMEM((K, TS, V), F32),
            pltpu.VMEM((2, GROUP, V), BF),
            pltpu.VMEM((2, GROUP, V), BF),
            pltpu.VMEM((2, 4, 7, CH, V), BF),
            pltpu.VMEM((2, 4, 7, CH, V), BF),
            pltpu.VMEM((2, 4, 2, CH, V), BF),
            pltpu.VMEM((2, 8, CH, V), BF),
            pltpu.VMEM((2, 4, CH, V), F32),
            pltpu.VMEM((2, 3, CH, V), F32),
            pltpu.VMEM((CH, V), BF),
            pltpu.VMEM((2 * V, V), F32),
            pltpu.VMEM((NCOL - 1, 8, V), F32),
            pltpu.VMEM((8, V), F32),
            pltpu.VMEM((G - 1, 8, V), F32),
            pltpu.VMEM((8, V), F32),
            pltpu.VMEM((2 * V, V), F32),
            pltpu.SemaphoreType.DMA((2, NSTAGE)),
            pltpu.SemaphoreType.DMA((2, NSTAGE, 8)),
            pltpu.SemaphoreType.DMA((2,)),
        ],
        compiler_params=pltpu.CompilerParams(
            collective_id=0, has_side_effects=True, vmem_limit_bytes=40 * 2**20
        ),
    )(vectors, tiles, tile_rows, tile_cols)


def solution(mesh):
    placed = (P("row", None), P(("row", "col"), None, None), P(("row", "col")), P(("row", "col")))
    return jax.shard_map(
        body,
        mesh=mesh,
        in_specs=placed,
        out_specs=(P(("row", "col"), None), P(("row", "col"), None), P(), P()),
        check_vma=False,
    )
```

time: 179 us -> 146 us (0.82)
  Pallas kernels: 172 us -> 139 us
    pallas_call x1, Pallas kernels: 172 us -> 139 us  [body(): pl.pallas_call(kernel, out_shape=(jax.ShapeDtypeStruct((CH, V), BF), jax....]
where the time goes in v2:
time: 146 us
  Pallas kernels  139 us (95%)
  local copies, waits for them, and re-layouts  6.14 us (4%)
    pallas_call x1, Pallas kernels, body(): pl.pallas_call(kernel, out_shape=(jax.ShapeDtypeStruct((CH, V), BF), jax....  139 us
    unnamed x12, local copies, waits for them, and re-layouts  6.14 us

profile of v2, /device:TPU:1, one launch (start us, length us, event | category | flops | bytes accessed | tf_op | source)
XLA Modules:
  0.0 145.9 jit_solution(2601290507492271869)
XLA Ops:
  0.6 0.0 copy-start
  0.6 1.2 copy-done
  1.9 0.0 copy-start.1
  1.9 1.1 copy-done.1
  3.0 0.0 copy-start.2
  3.0 0.7 copy-done.2
  3.6 0.0 copy-start.3
  3.6 0.7 copy-done.3
  4.3 139.1 %shard_map.75 = (bf16[96,128]{1,0:T(8,128)(2,1)S(1)}, bf16[96,128]{1,0:T(8,128)(2,1)S(1)}, f32[128,128]{1,0:T(8,128)S(1)}, f32[128,128]{1,0:T(8,128)S(1)}) custom-call(bf16[3072,128]{1,0:T(8,128)(2,1)S(1)} %copy-done.1, bf16[8,256,256]{2,1,0:T(8,128)(2,1)S(1)} %copy-done, s32[8]{0:T(128)S(1)} %copy-done.2, s32[8]{0:T(128)S(1)} %copy-done.3), custom_call_target="tpu_custom_call" | custom-call | tf_op jit(solution)/shard_map/pallas_call | solution.py:364
  143.4 0.6 copy.12
  144.0 0.6 copy.13
  144.6 0.6 copy.14
  145.3 0.6 copy.15
Async XLA Ops:
  0.6 1.2 copy-start
  1.9 1.1 copy-start.1
  3.0 0.7 copy-start.2
  3.6 0.7 copy-start.3

commit v3 on v2

--- a/solution.py
+++ b/solution.py
@@ -60,7 +60,8 @@
         pltpu.make_async_copy(ref, ref, sem).wait()
 
     def z_group(i):
-        return 4 * zl + (zh + 2 + i // 2) % 4, r + G * (i % 2)
+        j = i // 2
+        return 4 * zl + (zh + 2 - j + 3 * (j // 2) - 2 * (j // 3)) % 4, r + G * (i % 2)
 
     def z_owner(i):
         return p, 8 * y + i
@@ -78,6 +79,16 @@
 
     def pair_mate(j):
         return 4 * j + zh, 8 * zl + 2 * x1 + k
+
+    level, line = 8 * y + xk, 4 * zh + zl
+
+    def level_mate(i):
+        to = (level + i + 1) % 32
+        return to, 4 * (to // 8) + zh, 8 * zl + to % 8
+
+    def line_mate(i):
+        to = (line + i + 1) % 16
+        return 4 * y + to // 4, 8 * (to % 4) + xk
 
     barrier = pltpu.get_barrier_semaphore()
 
@@ -94,9 +105,8 @@
     loop(4, lambda q: greet_other(*out_owner(q, 0)))
     loop(4, lambda q: greet_other(*out_owner(q, 1)))
     loop(8, lambda i: greet_other(*out_source(i)))
-    loop(G - 1, lambda i: greet((r + i + 1) % G, c))
-    loop(4, lambda j: greet(*pair_mate(j)))
-    loop(NCOL - 1, lambda i: greet(r, (c + i + 1) % NCOL))
+    loop(15, lambda i: greet(*line_mate(i)))
+    loop(31, lambda i: greet(*level_mate(i)[1:]))
 
     straight = jnp.where(is_high, 0, 1)
     load_vec.wait()
@@ -148,13 +158,13 @@
     def z_in(a, src):
         loop(8, lambda i: send_or_copy(src, chunk(up[a], c), a, ZIN, xk, *z_group(i)))
 
-    def y_in(a):
+    def y_in(a, first, count):
         def forward(i):
-            part = chunk(up[a], 8 * y + i)
-            wait_bytes(part, rsem.at[a, ZIN, i])
+            part = chunk(up[a], 8 * y + first + i)
+            wait_bytes(part, rsem.at[a, ZIN, first + i])
             loop(3, lambda j: send(part, part, a, YIN, 0, 4 * ((y + j + 1) % 4) + zh, c))
 
-        loop(8, forward)
+        loop(count, forward)
 
     def to_mates(src, where):
         loop(7, lambda i: send(src, chunk(uo, where), 1, OX, 0, r, 8 * zl + (xk + i + 1) % 8))
@@ -209,23 +219,19 @@
         loop(4, pair)
         loop(3, mate)
 
-    def z_out(a):
+    def z_out(a, q):
         slot = zh * 2 + c // G
-
-        def step(q):
-            wait_bytes(yr.at[a, q], rsem.at[a, YRS, q])
-            acc = read(pb, a, 8 * q + to_xk)
-            for i in range(3):
-                acc = acc + yr[a, q, i].astype(F32)
-            zs[a, q, 0] = acc.astype(BF)
-            acc = yr[a, q, 3].astype(F32)
-            for i in range(4, 7):
-                acc = acc + yr[a, q, i].astype(F32)
-            zs[a, q, 1] = acc.astype(BF)
-            send_or_copy(zs.at[a, q, 0], zr.at[a, slot], a, ZOUT, 0, *out_owner(q, 0))
-            send_or_copy(zs.at[a, q, 1], zr.at[a, slot], a, ZOUT, 0, *out_owner(q, 1))
-
-        loop(4, step)
+        wait_bytes(yr.at[a, q], rsem.at[a, YRS, q])
+        acc = read(pb, a, 8 * q + to_xk)
+        for i in range(3):
+            acc = acc + yr[a, q, i].astype(F32)
+        zs[a, q, 0] = acc.astype(BF)
+        acc = yr[a, q, 3].astype(F32)
+        for i in range(4, 7):
+            acc = acc + yr[a, q, i].astype(F32)
+        zs[a, q, 1] = acc.astype(BF)
+        send_or_copy(zs.at[a, q, 0], zr.at[a, slot], a, ZOUT, 0, *out_owner(q, 0))
+        send_or_copy(zs.at[a, q, 1], zr.at[a, slot], a, ZOUT, 0, *out_owner(q, 1))
 
     def x_out(a, q):
         def mate(i):
@@ -265,35 +271,37 @@
 
     multiply(1, own_id, vec)
     loop(4, lambda q: gather(par_id, pb, 0, q))
-    waits = NCOL - 1 + G - 1 + 4 + 32
+    waits = 31 + 15 + 32
     pl.semaphore_wait(
         barrier, waits - 2 * jnp.where(self_z, 1, 0) - 2 * jnp.where(self_out, 1, 0)
     )
     z_in(0, chunk(vec, c))
     loop(4, lambda q: y_out(0, q))
-    z_out(0)
-    y_in(0)
+    loop(2, lambda q: z_out(0, q))
+    y_in(0, 0, 2)
+    z_out(0, 2)
+    y_in(0, 2, 2)
+    z_out(0, 3)
+    y_in(0, 4, 4)
     wait_bytes(up[0].at[pl.ds(0, 3 * QU)], rsem.at[0, YIN, 0])
     multiply(0, par_id, up[0])
 
-    def finish_own(a):
-        def step(i):
-            q = (zl + i + 1) % 4
-            gather(own_id, ob, a, q)
-            x_out(a, q)
-
-        loop(4, step)
-
-    finish_own(0)
+    def own_step(i):
+        q = (zl + i + 1) % 4
+        gather(own_id, ob, 0, q)
+        x_out(0, q)
+
+    loop(4, own_step)
     own_out(0)
     first = total(0)
     ach[...] = first
-    out1[...] = first
 
     z_in(1, ach)
     own_in()
+    out1[...] = first
     uo[pl.ds(pl.multiple_of(c * CH, CH), CH), :] = first
     gs[pl.ds(0, V), :] = inner(first, first)
+    y_in(1, 0, 8)
     wait_bytes(uo.at[pl.ds(0, 28 * CH)], rsem.at[1, OX, 0])
     multiply(1, own_id, uo)
 
@@ -302,37 +310,40 @@
         y_out(1, q)
 
     loop(4, partner_step)
-    y_in(1)
-    z_out(1)
     wait_bytes(up[1].at[pl.ds(0, 3 * QU)], rsem.at[1, YIN, 0])
+
+    gs[pl.ds(V, V), :] = inner(up[1][...], pb[1])
+
+    def gram_out(i):
+        to, row, col = level_mate(i)
+        send(gs.at[pl.ds(pl.multiple_of(to * 8, 8), 8)], gr1.at[i], 1, G1, 0, row, col)
+
+    loop(31, gram_out)
     multiply(0, par_id, up[1])
-    finish_own(1)
-
-    gs[pl.ds(V, V), :] = inner(uo[...], ob[1]) + inner(up[1][...], pb[1])
-
-    def gram_out(i):
-        to = (c + i + 1) % NCOL
-        send(gs.at[pl.ds(pl.multiple_of(to * 8, 8), 8)], gr1.at[i], 1, G1, 0, r, to)
-
-    loop(NCOL - 1, gram_out)
+
+    def both_step(i):
+        q = (zl + i + 1) % 4
+        gather(own_id, ob, 1, q)
+        x_out(1, q)
+        z_out(1, i)
+
+    loop(4, both_step)
+
+    wait_bytes(gr1, rsem.at[1, G1, 0])
+    mine = pl.ds(pl.multiple_of(level * 8, 8), 8)
+    gp[...] = lax.fori_loop(0, 31, lambda i, s: s + gr1[i], gs[mine, :])
+    loop(15, lambda i: send(gp, gr2.at[i], 1, G2, 0, *line_mate(i)))
     own_out(1)
-
-    wait_bytes(gr1, rsem.at[1, G1, 0])
-    acc = gs[pl.ds(pl.multiple_of(c * 8, 8), 8), :]
-    gp[...] = lax.fori_loop(0, NCOL - 1, lambda i, s: s + gr1[i], acc)
-    loop(G - 1, lambda i: send(gp, gr2.at[i], 1, G2, 0, (r + i + 1) % G, c))
-    second = total(1)
-    out2[...] = second
-
     wait_bytes(gr2, rsem.at[1, G2, 0])
-    acc = lax.fori_loop(0, G - 1, lambda i, s: s + gr2[i], gp[...])
+    acc = lax.fori_loop(0, 15, lambda i, s: s + gr2[i], gp[...])
     gf[...] = acc
-    mine = pl.ds(pl.multiple_of(c * 8, 8), 8)
-    loop(NCOL - 1, lambda i: send(gf, ga.at[mine], 1, G3, 0, r, (c + i + 1) % NCOL))
+    loop(31, lambda i: send(gf, ga.at[mine], 1, G3, 0, *level_mate(i)[1:]))
     ga[mine, :] = acc
+    out2[...] = total(1)
     wait_bytes(ga.at[pl.ds(0, 2 * V - 8)], rsem.at[1, G3, 0])
     gn[...] = ga[pl.ds(0, V), :] / NROWS
-    gr[...] = ga[pl.ds(V, V), :] / NROWS
+    half = ga[pl.ds(V, V), :]
+    gr[...] = (half + half.T) / NROWS
 
     def sent(a, stage, less, chunks):
         @pl.when(less)
@@ -399,7 +410,7 @@
             pltpu.SemaphoreType.DMA((2,)),
         ],
         compiler_params=pltpu.CompilerParams(
-            collective_id=0, has_side_effects=True, vmem_limit_bytes=40 * 2**20
+            collective_id=0, has_side_effects=True, vmem_limit_bytes=64 * 2**20
         ),
     )(vectors, tiles, tile_rows, tile_cols)
 

time: 146 us -> 127 us (0.87)
  Pallas kernels: 139 us -> 122 us
  local copies, waits for them, and re-layouts: 6.14 us -> 4.22 us
    pallas_call x1, Pallas kernels: 139 us -> 122 us  [body(): pl.pallas_call(kernel, out_shape=(jax.ShapeDtypeStruct((CH, V), BF), jax....]
    unnamed x12 -> x8, local copies, waits for them, and re-layouts: 6.14 us -> 4.22 us
where the time goes in v3:
time: 127 us; the launch traced here: 126 us
  Pallas kernels  122 us (96%)
  local copies, waits for them, and re-layouts  4.22 us (3%)
    pallas_call x1, Pallas kernels, body(): pl.pallas_call(kernel, out_shape=(jax.ShapeDtypeStruct((CH, V), BF), jax....  122 us
    unnamed x8, local copies, waits for them, and re-layouts  4.22 us

profile of v3, /device:TPU:1, one launch (start us, length us, event | category | flops | bytes accessed | tf_op | source)
XLA Modules:
  0.0 126.5 jit_solution(15569985929485268540)
XLA Ops:
  0.6 121.6 %shard_map.75 = (bf16[96,128]{1,0:T(8,128)(2,1)}, bf16[96,128]{1,0:T(8,128)(2,1)}, f32[128,128]{1,0:T(8,128)}, f32[128,128]{1,0:T(8,128)}) custom-call(bf16[3072,128]{1,0:T(8,128)(2,1)} %vec_in.1, bf16[8,256,256]{2,1,0:T(8,128)(2,1)} %tiles_in.1, s32[8]{0:T(128)} %trows.1, s32[8]{0:T(128)} %tcols.1), custom_call_target="tpu_custom_call" | custom-call | tf_op jit(solution)/shard_map/pallas_call | solution.py:375
  122.2 0.0 copy-start.1
  122.2 1.4 %copy.12 = bf16[96,128]{1,0:T(8,128)(2,1)} copy(bf16[96,128]{1,0:T(8,128)(2,1)} %get-tuple-element.8) | data formatting | bytes 49152
  123.6 1.3 %copy.13 = bf16[96,128]{1,0:T(8,128)(2,1)} copy(bf16[96,128]{1,0:T(8,128)(2,1)} %get-tuple-element.9) | data formatting | bytes 49152
  125.0 0.0 copy-done.1
  125.0 0.0 copy-start
  125.0 0.6 copy.14
  125.6 0.2 copy-done
  125.8 0.6 copy.15
Async XLA Ops:
  122.2 2.7 %copy-start.1 = (f32[128,128]{1,0:T(8,128)S(1)}, f32[128,128]{1,0:T(8,128)}, u32[]{:S(2)}) copy-start(f32[128,128]{1,0:T(8,128)} %get-tuple-element.10) | copy-start | bytes 196612
  125.0 0.9 copy-start

commit v4 on v3

--- a/solution.py
+++ b/solution.py
@@ -19,8 +19,8 @@
 QU = GROUP // 4
 NROWS = GROUP * G
 
-ZIN, YIN, YRS, ZOUT, OZ, OX, XRS, OOUT, G1, G2, G3 = range(11)
-NSTAGE = 11
+ZIN, YIN, YRS, ZOUT, OZ, OX, SIB, XRS, OOUT, G1, G2, G3 = range(12)
+NSTAGE = 12
 
 
 def loop(n, body):
@@ -33,7 +33,7 @@
 
 def kernel(
     vec_in, tiles_in, trows, tcols, out1, out2, gn, gr,
-    vec, tiles, tt, up0, up1, uo, prod, pb, ob, yr, xr, zs, zr, osum, orr, ach,
+    vec, tiles, tt, up0, up1, uo, prod, pb, ob, yr, sib, xs, xr, zs, zr, osum, orr, ach,
     gs, gr1, gp, gr2, gf, ga, ssem, rsem, lsem,
 ):
     up = (up0, up1)
@@ -201,7 +201,7 @@
                 acc = prod[0, piece, :] * weights[0]
                 for k in range(1, K):
                     acc = acc + prod[k, piece, :] * weights[k]
-                target[a, pl.ds(pl.multiple_of(b * TS + 64 * s, 64), 64), :] = acc.astype(BF)
+                target[a, pl.ds(pl.multiple_of(b * TS + 64 * s, 64), 64), :] = acc.astype(target.dtype)
 
         loop(3, block)
 
@@ -233,17 +233,27 @@
         send_or_copy(zs.at[a, q, 0], zr.at[a, slot], a, ZOUT, 0, *out_owner(q, 0))
         send_or_copy(zs.at[a, q, 1], zr.at[a, slot], a, ZOUT, 0, *out_owner(q, 1))
 
+    def pair_out(a, q):
+        def piece(i):
+            part = chunk(ob.at[a], 8 * q + 2 * i + 1 - k)
+            send(part, sib.at[a, q, i], a, SIB, q, r, 8 * zl + 2 * x + 1 - k)
+
+        loop(4, piece)
+
     def x_out(a, q):
+        wait_bytes(sib.at[a, q], rsem.at[a, SIB, q])
+
         def mate(i):
-            to = (xk + i + 1) % 8
-            send(chunk(ob.at[a], 8 * q + to), xr.at[a, q, i], a, XRS, q, r, 8 * zl + to)
-
-        loop(7, mate)
+            to = (x + i + 1) % 4
+            xs[a, q, i] = (read(ob, a, 8 * q + 2 * to + k) + sib[a, q, to]).astype(BF)
+            send(xs.at[a, q, i], xr.at[a, q, i], a, XRS, q, r, 8 * zl + 2 * to + k)
+
+        loop(3, mate)
 
     def own_sum(a, q):
+        acc = read(ob, a, 8 * q + xk) + sib[a, q, x]
         wait_bytes(xr.at[a, q], rsem.at[a, XRS, q])
-        acc = read(ob, a, 8 * q + xk)
-        for i in range(7):
+        for i in range(3):
             acc = acc + xr[a, q, i].astype(F32)
         osum[a, q] = acc
 
@@ -286,12 +296,24 @@
     wait_bytes(up[0].at[pl.ds(0, 3 * QU)], rsem.at[0, YIN, 0])
     multiply(0, par_id, up[0])
 
-    def own_step(i):
-        q = (zl + i + 1) % 4
-        gather(own_id, ob, 0, q)
-        x_out(0, q)
-
-    loop(4, own_step)
+    def nth(i):
+        return (zl + i + 1) % 4
+
+    def own_gather(a, i):
+        gather(own_id, ob, a, nth(i))
+        pair_out(a, nth(i))
+
+    def own_products(a):
+        own_gather(a, 0)
+
+        def step(i):
+            own_gather(a, i + 1)
+            x_out(a, nth(i))
+
+        loop(3, step)
+        x_out(a, nth(3))
+
+    own_products(0)
     own_out(0)
     first = total(0)
     ach[...] = first
@@ -321,18 +343,12 @@
     loop(31, gram_out)
     multiply(0, par_id, up[1])
 
-    def both_step(i):
-        q = (zl + i + 1) % 4
-        gather(own_id, ob, 1, q)
-        x_out(1, q)
-        z_out(1, i)
-
-    loop(4, both_step)
-
+    own_products(1)
     wait_bytes(gr1, rsem.at[1, G1, 0])
     mine = pl.ds(pl.multiple_of(level * 8, 8), 8)
     gp[...] = lax.fori_loop(0, 31, lambda i, s: s + gr1[i], gs[mine, :])
     loop(15, lambda i: send(gp, gr2.at[i], 1, G2, 0, *line_mate(i)))
+    loop(4, lambda q: z_out(1, q))
     own_out(1)
     wait_bytes(gr2, rsem.at[1, G2, 0])
     acc = lax.fori_loop(0, 15, lambda i, s: s + gr2[i], gp[...])
@@ -359,6 +375,7 @@
         sent(a, ZOUT, self_out, 8)
         wait_bytes(up[a].at[pl.ds(0, 24 * CH)], ssem.at[a, YIN])
         wait_bytes(yr.at[a], ssem.at[a, YRS])
+        wait_bytes(sib.at[a], ssem.at[a, SIB])
         wait_bytes(xr.at[a], ssem.at[a, XRS])
         wait_bytes(orr.at[a], ssem.at[a, OOUT])
     wait_bytes(uo.at[pl.ds(0, 3 * CH)], ssem.at[1, OZ])
@@ -368,18 +385,24 @@
     wait_bytes(gr1, ssem.at[1, G3])
 
 
+def hand_over(*refs):
+    for i in range(4):
+        refs[4 + i][...] = refs[i][...]
+
+
 def body(vectors, tiles, tile_rows, tile_cols):
     vmem = pl.BlockSpec(memory_space=pltpu.VMEM)
     smem = pl.BlockSpec(memory_space=pltpu.SMEM)
     hbm = pl.BlockSpec(memory_space=pltpu.HBM)
-    return pl.pallas_call(
+    outs = (
+        jax.ShapeDtypeStruct((CH, V), BF),
+        jax.ShapeDtypeStruct((CH, V), BF),
+        jax.ShapeDtypeStruct((V, V), F32),
+        jax.ShapeDtypeStruct((V, V), F32),
+    )
+    results = pl.pallas_call(
         kernel,
-        out_shape=(
-            jax.ShapeDtypeStruct((CH, V), BF),
-            jax.ShapeDtypeStruct((CH, V), BF),
-            jax.ShapeDtypeStruct((V, V), F32),
-            jax.ShapeDtypeStruct((V, V), F32),
-        ),
+        out_shape=outs,
         in_specs=[hbm, hbm, smem, smem],
         out_specs=(vmem,) * 4,
         scratch_shapes=[
@@ -391,9 +414,11 @@
             pltpu.VMEM((GROUP, V), BF),
             pltpu.VMEM((K, TS, V), F32),
             pltpu.VMEM((2, GROUP, V), BF),
-            pltpu.VMEM((2, GROUP, V), BF),
+            pltpu.VMEM((2, GROUP, V), F32),
             pltpu.VMEM((2, 4, 7, CH, V), BF),
-            pltpu.VMEM((2, 4, 7, CH, V), BF),
+            pltpu.VMEM((2, 4, 4, CH, V), F32),
+            pltpu.VMEM((2, 4, 3, CH, V), BF),
+            pltpu.VMEM((2, 4, 3, CH, V), BF),
             pltpu.VMEM((2, 4, 2, CH, V), BF),
             pltpu.VMEM((2, 8, CH, V), BF),
             pltpu.VMEM((2, 4, CH, V), F32),
@@ -413,6 +438,13 @@
             collective_id=0, has_side_effects=True, vmem_limit_bytes=64 * 2**20
         ),
     )(vectors, tiles, tile_rows, tile_cols)
+    return pl.pallas_call(
+        hand_over,
+        out_shape=outs,
+        in_specs=[vmem] * 4,
+        out_specs=(vmem,) * 4,
+        compiler_params=pltpu.CompilerParams(vmem_limit_bytes=64 * 2**20),
+    )(*results)
 
 
 def solution(mesh):

time: 127 us -> 121 us (0.953)
  local copies, waits for them, and re-layouts: 4.22 us -> 0 us
  Pallas kernels: 122 us -> 120 us
    unnamed x8 -> x0, local copies, waits for them, and re-layouts: 4.22 us -> none
    pallas_call x1 -> x2, Pallas kernels: 122 us -> 120 us  [the longest x1 119 us: body(): pl.pallas_call(kernel, out_shape=outs, in_specs=[hbm, hbm, smem, smem], o...]
where the time goes in v4:
time: 121 us
  Pallas kernels  120 us (99%)
    pallas_call x1, Pallas kernels, body(): pl.pallas_call(kernel, out_shape=outs, in_specs=[hbm, hbm, smem, smem], o...  119 us

profile of v4, /device:TPU:1, one launch (start us, length us, event | category | flops | bytes accessed | tf_op | source)
XLA Modules:
  0.0 120.9 jit_solution(14879755099187820500)
XLA Ops:
  0.6 118.7 %shard_map.75 = (bf16[96,128]{1,0:T(8,128)(2,1)}, bf16[96,128]{1,0:T(8,128)(2,1)}, f32[128,128]{1,0:T(8,128)}, f32[128,128]{1,0:T(8,128)}) custom-call(bf16[3072,128]{1,0:T(8,128)(2,1)} %vec_in.1, bf16[8,256,256]{2,1,0:T(8,128)(2,1)} %tiles_in.1, s32[8]{0:T(128)} %trows.1, s32[8]{0:T(128)} %tcols.1), custom_call_target="tpu_custom_call" | custom-call | tf_op jit(solution)/shard_map/pallas_call | solution.py:403
  119.3 1.6 %shard_map.76 = (bf16[96,128]{1,0:T(8,128)(2,1)}, bf16[96,128]{1,0:T(8,128)(2,1)}, f32[128,128]{1,0:T(8,128)}, f32[128,128]{1,0:T(8,128)}) custom-call(bf16[96,128]{1,0:T(8,128)(2,1)} %get-tuple-element.8.refs_0_, bf16[96,128]{1,0:T(8,128)(2,1)} %get-tuple-element.9.refs_1_, f32[128,128]{1,0:T(8,128)} %get-tuple-element.10.refs_2_, ...), custom_call_target="tpu_custom_call" | custom-call | tf_op jit(solution)/shard_map/pallas_call | solution.py:441

commit v5 on v4

--- a/solution.py
+++ b/solution.py
@@ -329,7 +329,6 @@
 
     def partner_step(q):
         gather(par_id, pb, 1, q)
-        y_out(1, q)
 
     loop(4, partner_step)
     wait_bytes(up[1].at[pl.ds(0, 3 * QU)], rsem.at[1, YIN, 0])
@@ -341,6 +340,7 @@
         send(gs.at[pl.ds(pl.multiple_of(to * 8, 8), 8)], gr1.at[i], 1, G1, 0, row, col)
 
     loop(31, gram_out)
+    loop(4, lambda q: y_out(1, q))
     multiply(0, par_id, up[1])
 
     own_products(1)

time: 121 us -> 118 us (0.975)
  Pallas kernels: 120 us -> 117 us
    pallas_call x1, Pallas kernels: 119 us -> 115 us  [body(): pl.pallas_call(kernel, out_shape=outs, in_specs=[hbm, hbm, smem, smem], o...]
where the time goes in v5:
time: 118 us
  Pallas kernels  117 us (99%)
    pallas_call x1, Pallas kernels, body(): pl.pallas_call(kernel, out_shape=outs, in_specs=[hbm, hbm, smem, smem], o...  115 us

profile of v5, /device:TPU:1, one launch (start us, length us, event | category | flops | bytes accessed | tf_op | source)
XLA Modules:
  0.0 117.5 jit_solution(8635740713847001540)
XLA Ops:
  0.6 115.3 %shard_map.75 = (bf16[96,128]{1,0:T(8,128)(2,1)}, bf16[96,128]{1,0:T(8,128)(2,1)}, f32[128,128]{1,0:T(8,128)}, f32[128,128]{1,0:T(8,128)}) custom-call(bf16[3072,128]{1,0:T(8,128)(2,1)} %vec_in.1, bf16[8,256,256]{2,1,0:T(8,128)(2,1)} %tiles_in.1, s32[8]{0:T(128)} %trows.1, s32[8]{0:T(128)} %tcols.1), custom_call_target="tpu_custom_call" | custom-call | tf_op jit(solution)/shard_map/pallas_call | solution.py:403
  115.9 1.6 %shard_map.76 = (bf16[96,128]{1,0:T(8,128)(2,1)}, bf16[96,128]{1,0:T(8,128)(2,1)}, f32[128,128]{1,0:T(8,128)}, f32[128,128]{1,0:T(8,128)}) custom-call(bf16[96,128]{1,0:T(8,128)(2,1)} %get-tuple-element.8.refs_0_, bf16[96,128]{1,0:T(8,128)(2,1)} %get-tuple-element.9.refs_1_, f32[128,128]{1,0:T(8,128)} %get-tuple-element.10.refs_2_, ...), custom_call_target="tpu_custom_call" | custom-call | tf_op jit(solution)/shard_map/pallas_call | solution.py:441

commit v6 on v5

--- a/solution.py
+++ b/solution.py
@@ -19,8 +19,8 @@
 QU = GROUP // 4
 NROWS = GROUP * G
 
-ZIN, YIN, YRS, ZOUT, OZ, OX, SIB, XRS, OOUT, G1, G2, G3 = range(12)
-NSTAGE = 12
+ZIN, YIN, YRS, ZOUT, OZ, OX, OS, SIB, XRS, OOUT, G1, G2, G3 = range(13)
+NSTAGE = 13
 
 
 def loop(n, body):
@@ -166,20 +166,35 @@
 
         loop(count, forward)
 
-    def to_mates(src, where):
-        loop(7, lambda i: send(src, chunk(uo, where), 1, OX, 0, r, 8 * zl + (xk + i + 1) % 8))
+    def to_sibling(src, where):
+        send(src, chunk(uo, where), 1, OS, 0, r, c + 1 - 2 * k)
+
+    def spread(src, where, group):
+        loop(3, lambda i: send(src, chunk(uo, where), 1, OX, group, r, 8 * zl + 2 * ((x + i + 1) % 4) + k))
+        to_sibling(src, where)
 
     def own_in():
         loop(3, lambda i: send(ach, chunk(uo, c), 1, OZ, i, r, 8 * ((zl + i + 1) % 4) + xk))
-        to_mates(ach, c)
+        spread(ach, c, 0)
 
         def forward(i):
             cc = 8 * ((zl + 3 - i) % 4) + xk
             part = chunk(uo, cc)
             wait_bytes(part, rsem.at[1, OZ, i])
-            to_mates(part, cc)
+            spread(part, cc, 1 + i)
 
         loop(3, forward)
+
+        def across(g):
+            wait_bytes(uo.at[pl.ds(0, 3 * CH)], rsem.at[1, OX, g])
+
+            def one(i):
+                cc = 8 * ((zl + 4 - g) % 4) + 2 * ((x + i + 1) % 4) + k
+                to_sibling(chunk(uo, cc), cc)
+
+            loop(3, one)
+
+        return across
 
     def one_if_same(left, right):
         gap = left - right
@@ -319,12 +334,13 @@
     ach[...] = first
 
     z_in(1, ach)
-    own_in()
+    across = own_in()
     out1[...] = first
     uo[pl.ds(pl.multiple_of(c * CH, CH), CH), :] = first
     gs[pl.ds(0, V), :] = inner(first, first)
     y_in(1, 0, 8)
-    wait_bytes(uo.at[pl.ds(0, 28 * CH)], rsem.at[1, OX, 0])
+    loop(4, across)
+    wait_bytes(uo.at[pl.ds(0, 16 * CH)], rsem.at[1, OS, 0])
     multiply(1, own_id, uo)
 
     def partner_step(q):
@@ -379,7 +395,8 @@
         wait_bytes(xr.at[a], ssem.at[a, XRS])
         wait_bytes(orr.at[a], ssem.at[a, OOUT])
     wait_bytes(uo.at[pl.ds(0, 3 * CH)], ssem.at[1, OZ])
-    wait_bytes(uo.at[pl.ds(0, 28 * CH)], ssem.at[1, OX])
+    wait_bytes(uo.at[pl.ds(0, 12 * CH)], ssem.at[1, OX])
+    wait_bytes(uo.at[pl.ds(0, 16 * CH)], ssem.at[1, OS])
     wait_bytes(gr1, ssem.at[1, G1])
     wait_bytes(gr2, ssem.at[1, G2])
     wait_bytes(gr1, ssem.at[1, G3])

time: 118 us -> 117 us (level)
  no operation moved by 1% of the time
where the time goes in v6:
time: 117 us
  Pallas kernels  116 us (99%)
    pallas_call x1, Pallas kernels, body(): pl.pallas_call(kernel, out_shape=outs, in_specs=[hbm, hbm, smem, smem], o...  115 us

profile of v6, /device:TPU:1, one launch (start us, length us, event | category | flops | bytes accessed | tf_op | source)
XLA Modules:
  0.0 116.9 jit_solution(16919944383354070216)
XLA Ops:
  0.6 114.7 %shard_map.75 = (bf16[96,128]{1,0:T(8,128)(2,1)}, bf16[96,128]{1,0:T(8,128)(2,1)}, f32[128,128]{1,0:T(8,128)}, f32[128,128]{1,0:T(8,128)}) custom-call(bf16[3072,128]{1,0:T(8,128)(2,1)} %vec_in.1, bf16[8,256,256]{2,1,0:T(8,128)(2,1)} %tiles_in.1, s32[8]{0:T(128)} %trows.1, s32[8]{0:T(128)} %tcols.1), custom_call_target="tpu_custom_call" | custom-call | tf_op jit(solution)/shard_map/pallas_call | solution.py:420
  115.3 1.6 %shard_map.76 = (bf16[96,128]{1,0:T(8,128)(2,1)}, bf16[96,128]{1,0:T(8,128)(2,1)}, f32[128,128]{1,0:T(8,128)}, f32[128,128]{1,0:T(8,128)}) custom-call(bf16[96,128]{1,0:T(8,128)(2,1)} %get-tuple-element.8.refs_0_, bf16[96,128]{1,0:T(8,128)(2,1)} %get-tuple-element.9.refs_1_, f32[128,128]{1,0:T(8,128)} %get-tuple-element.10.refs_2_, ...), custom_call_target="tpu_custom_call" | custom-call | tf_op jit(solution)/shard_map/pallas_call | solution.py:458
